TPU v7x, 512 devices: a whole 4x4x16 slice. The times are simulated.
512 devices in a mesh: feat: 8 (over x, core), vert: 64 (over y, z).
Axes of the slice: x: 4, y: 4, z: 16, core: 2. Of those that a mesh axis runs over, the one named last changes fastest.
Arguments:
- features: bfloat16 [512, 131072], P('feat', 'vert'), may hold values from -6 to 6
- tiles: bfloat16 [64, 56, 128, 128], P('vert'), may hold values from -0.375 to 0.375
- tile_rows: int32 [64, 56], P('vert'), may hold values from 0 to 15, as said below
- tile_cols: int32 [64, 56], P('vert'), may hold values from 0 to 1023, as said below
- tile_counts: int32 [64], P('vert'), may hold values from 1 to 56, as said below
- weight: bfloat16 [512, 512], replicated, may hold values from -0.25 to 0.25
- output_gradient: bfloat16 [512, 131072], P(None, ('vert', 'feat')), may hold values from -6 to 6
Outputs:
- activation: bfloat16 [512, 131072], P(None, ('vert', 'feat'))
- weight_gradient: float32 [512, 512], replicated
- feature_grad: bfloat16 [512, 131072], P('feat', 'vert')
Inputs may be any that keep to these rules, and one draw needn't show every extreme that they name: `tile_rows`: slots at or beyond a block's count are unused; their tiles and indices are arbitrary. The block of a column tile, tile_cols // 16, equals the slot's own block or differs from it in exactly one of the lowest 4 bits. `tile_counts`: some block uses all 56 slots.
All inputs are finite; a program needn't handle non-finite values.
Results may differ from a plain program's by a relative error of at most 0.02.
Values may be sent and summed in bfloat16 or wider, within the bound.
A program may use at most 64 MiB of HBM per device.

v0:
```python
import jax
import jax.numpy as jnp
from jax import lax
from jax.sharding import PartitionSpec as P

LEVELS = 4


def partner(shard, axis, stride):
    return lax.ppermute(shard, axis, [(i, i ^ 1 << stride) for i in range(lax.axis_size(axis))])


def fetch_partners(features):
    fetched = []
    for bit in range(LEVELS):
        fetched.append(partner(features, "vert", bit))
    return fetched


def send_partials(remote_terms):
    received = []
    for bit in range(LEVELS):
        outgoing = remote_terms[:, bit].astype(jnp.bfloat16)
        received.append(partner(outgoing, "vert", bit).astype(jnp.float32))
    return received


def tile_products(stacked, level, local, rows, block_tiles, weights, row_tiles):
    picked = stacked[level, :, local]
    share_value = jnp.einsum(
        "cfk,crk->cfr", picked, block_tiles, preferred_element_type=jnp.float32
    )
    indicator_matrix = (rows[None, :] == jnp.arange(row_tiles, dtype=jnp.int32)[:, None]).astype(
        jnp.float32
    ) * weights[None, :]
    reduced_total = jnp.einsum("zy,yqw->qzw", indicator_matrix, share_value)
    return reduced_total.reshape(stacked.shape[1], row_tiles * stacked.shape[3])


def position_summands(share_value, slot_index, groups, feat_local, vdev):
    targets = jnp.arange(groups * (vdev // share_value.shape[2]), dtype=jnp.int32)
    placing = (slot_index[None, :] == targets[:, None]).astype(jnp.float32)
    return jnp.einsum("sc,cfk->fsk", placing, share_value).reshape(feat_local, groups, vdev)


def body(features, tiles, tile_rows, tile_cols, tile_counts, weight, output_gradient):
    feat_local, vdev = features.shape
    tile_side = tiles.shape[2]
    slot_count = tiles.shape[1]
    row_tiles = vdev // tile_side
    my_block = lax.axis_index("vert")
    block_tiles = tiles[0]
    rows = tile_rows[0]
    cols = tile_cols[0]
    differ = jnp.bitwise_xor(cols // row_tiles, my_block)
    level = jnp.zeros(cols.shape, jnp.int32)
    for bit in range(LEVELS):
        level = level + jnp.where(differ == 1 << bit, bit + 1, 0).astype(jnp.int32)
    local = cols % row_tiles
    valid = (jnp.arange(slot_count, dtype=jnp.int32) < tile_counts[0]).astype(jnp.float32)
    stacked = jnp.stack([features] + fetch_partners(features)).reshape(
        LEVELS + 1, feat_local, row_tiles, tile_side
    )
    aggregated = tile_products(stacked, level, local, rows, block_tiles, valid, row_tiles).astype(
        jnp.bfloat16
    )
    full_rows = lax.all_to_all(aggregated, "feat", split_axis=1, concat_axis=0, tiled=True)
    pre = jnp.einsum("io,iv->ov", weight, full_rows, preferred_element_type=jnp.float32)
    sigma = jax.nn.sigmoid(pre)
    activation = (pre * sigma).astype(jnp.bfloat16)
    pre_grad = (output_gradient.astype(jnp.float32) * sigma * (1.0 + pre * (1.0 - sigma))).astype(
        jnp.bfloat16
    )
    weight_term = jnp.einsum("iv,ov->io", full_rows, pre_grad, preferred_element_type=jnp.float32)
    weight_gradient = lax.psum(weight_term, ("feat", "vert"))
    agg_grad = jnp.einsum("io,ov->iv", weight, pre_grad, preferred_element_type=jnp.float32).astype(
        jnp.bfloat16
    )
    grad_cols = lax.all_to_all(agg_grad, "feat", split_axis=0, concat_axis=1, tiled=True)
    picked = grad_cols.reshape(feat_local, row_tiles, tile_side)[:, rows, :]
    share_value = (
        jnp.einsum("fcr,crk->cfk", picked, block_tiles, preferred_element_type=jnp.float32)
        * valid[:, None, None]
    )
    spread = position_summands(share_value, level * row_tiles + local, LEVELS + 1, feat_local, vdev)
    received = send_partials(spread[:, 1:])
    feature_grad = spread[:, 0]
    for term in received:
        feature_grad = feature_grad + term
    return (activation, weight_gradient, feature_grad.astype(jnp.bfloat16))


def solution(mesh):
    in_specs = (
        P("feat", "vert"),
        P("vert", None, None, None),
        P("vert", None),
        P("vert", None),
        P("vert"),
        P(),
        P(None, ("vert", "feat")),
    )
    out_specs = (P(None, ("vert", "feat")), P(), P("feat", "vert"))
    return jax.shard_map(body, mesh=mesh, in_specs=in_specs, out_specs=out_specs, check_vma=False)
```

profile of v0, /device:TPU:1, one launch (start us, length us, event | category | flops | bytes accessed | tf_op | source)
XLA Modules:
  0.0 628.8 jit_solution(14471863540489969215)
XLA Ops:
  7.2 0.0 copy-start
  7.2 5.9 collective-permute-start.1
  13.1 3.5 collective-permute-start
  16.6 12.7 %collective-permute-start.3 = (bf16[64,2048]{1,0:T(8,128)(2,1)}, bf16[64,2048]{1,0:T(8,128)(2,1)S(1)}, u32[]{:S(2)}, u32[]{:S(2)}) collective-permute-start(bf16[64,2048]{1,0:T(8,128)(2,1)} %param.7), channel_id=1, source_target_pairs={{0,8},{1,9},{2,10},{3,11},{4,12},{5,13},{6,14},{7,15},{8,0},{9,1},... | collective-permute-start | bytes 786440 | tf_op jit(solution)/shard_map/ppermute | solution.py:10
  29.4 4.0 collective-permute-start.2
  34.0 0.7 fusion.49
  34.7 1.0 copy.87
  35.7 0.8 copy_dynamic-update-slice_fusion.4
  36.5 0.0 collective-permute-done.1
  36.5 0.0 collective-permute-done
  36.6 10.2 %collective-permute-done.3 = bf16[64,2048]{1,0:T(8,128)(2,1)S(1)} collective-permute-done((bf16[64,2048]{1,0:T(8,128)(2,1)}, bf16[64,2048]{1,0:T(8,128)(2,1)S(1)}, u32[]{:S(2)}, u32[]{:S(2)}) %collective-permute-start.3) | collective-permute-done | bytes 262176 | tf_op jit(solution)/shard_map/ppermute | solution.py:10
  46.9 31.9 %collective-permute-done.2 = bf16[64,2048]{1,0:T(8,128)(2,1)S(1)} collective-permute-done((bf16[64,2048]{1,0:T(8,128)(2,1)}, bf16[64,2048]{1,0:T(8,128)(2,1)S(1)}, u32[]{:S(2)}, u32[]{:S(2)}) %collective-permute-start.2) | collective-permute-done | bytes 262176 | tf_op jit(solution)/shard_map/ppermute | solution.py:10
  78.8 0.8 copy_dynamic-update-slice_fusion.3
  79.5 0.8 copy_dynamic-update-slice_fusion.2
  80.3 0.8 copy_dynamic-update-slice_fusion.1
  81.0 0.8 copy_dynamic-update-slice_fusion
  81.8 2.2 gather_fusion
  84.0 0.0 copy-done
  84.0 0.0 copy-start.3
  84.1 1.4 fusion.2
  85.4 0.0 copy-done.3
  85.4 0.0 copy-start.2
  85.4 0.6 fusion.18
  86.0 0.1 convert_element_type.72
  86.1 0.8 copy.75
  86.9 4.8 all-to-all-start
  91.7 0.0 copy-done.2
  91.7 0.1 copy.76
  91.8 6.3 %all-to-all-done = bf16[64,8,256]{2,0,1:T(8,128)(2,1)S(1)} async-done(((bf16[64,8,256]{2,0,1:T(8,128)(2,1)}), bf16[64,8,256]{2,0,1:T(8,128)(2,1)S(1)}, u32[]{:S(2)}, u32[]{:S(2)}) %all-to-all-start) | async-done | bytes 262176 | tf_op jit(solution)/shard_map/all_to_all | solution.py:67
  98.2 0.0 copy-done.1
  98.2 1.2 multiply_convert_fusion
  99.4 0.3 fusion.17
  99.7 0.8 copy.77
  100.6 4.4 all-to-all-start.1
  104.9 0.0 all-reduce.2.cloned.1.call-start
  105.0 6.5 %all-to-all-done.1 = bf16[8,64,256]{2,1,0:T(8,128)(2,1)S(1)} async-done(((bf16[8,64,256]{2,1,0:T(8,128)(2,1)}), bf16[8,64,256]{2,1,0:T(8,128)(2,1)S(1)}, u32[]{:S(2)}, u32[]{:S(2)}) %all-to-all-start.1) | async-done | bytes 262176 | tf_op jit(solution)/shard_map/all_to_all | solution.py:79
  111.5 0.1 copy.78
  111.6 0.1 reshape.231
  111.7 0.1 copy.79
  111.8 0.7 gather_fusion.1
  112.5 0.6 fusion.11
  113.1 2.4 fusion.8
  115.5 4.4 reshape.232
  119.9 2.5 convert.6
  122.4 1.9 fusion.51
  124.3 0.2 copy.115
  124.5 0.2 copy.112
  124.6 0.9 copy.113
  125.5 0.9 copy.114
  126.3 1.9 collective-permute-start.5
  128.3 1.9 collective-permute-start.6
  130.2 8.5 %collective-permute-start.7 = (bf16[64,2048]{1,0:T(8,128)(2,1)S(1)}, bf16[64,2048]{1,0:T(8,128)(2,1)}, u32[]{:S(2)}, u32[]{:S(2)}) collective-permute-start(bf16[64,2048]{1,0:T(8,128)(2,1)S(1)} %bitcast.108), channel_id=1, source_target_pairs={{0,8},{1,9},{2,10},{3,11},{4,12},{5,13},{6,14},{7,15},{8,0},{9,1},... | collective-permute-start | bytes 786440 | tf_op jit(solution)/shard_map/ppermute | solution.py:10
  138.7 5.8 collective-permute-start.4
  144.5 1.3 fusion.52
  145.8 0.0 all-reduce.2.cloned.1.call-update
  145.8 1.8 copy.81
  147.7 0.0 collective-permute-done.5
  147.7 33.5 %collective-permute-done.6 = bf16[64,2048]{1,0:T(8,128)(2,1)} collective-permute-done((bf16[64,2048]{1,0:T(8,128)(2,1)}, bf16[64,2048]{1,0:T(8,128)(2,1)}, u32[]{:S(2)}, u32[]{:S(2)}) %collective-permute-start.6) | collective-permute-done | bytes 262176 | tf_op jit(solution)/shard_map/ppermute | solution.py:10
  181.1 0.0 collective-permute-done.7
  181.1 0.0 collective-permute-done.4
  181.1 0.0 slice-done
  181.2 2.2 fusion.25
  183.3 436.4 %all-reduce.2.cloned.1.call-done = f32[512,512]{1,0:T(8,128)} async-done(((f32[512,512]{1,0:T(8,128)}), f32[512,512]{1,0:T(8,128)}) %all-reduce.2.cloned.1.call-update) | async-done | bytes 1048592 | tf_op jit(solution)/shard_map/psum | solution.py:75
  619.7 2.3 copy.122
  (12 shorter events, 0.2 us)
Async XLA Ops:
  7.2 76.9 %copy-start = (bf16[1,56,128,128]{3,2,1,0:T(8,128)(2,1)S(1)}, bf16[1,56,128,128]{3,2,1,0:T(8,128)(2,1)}, u32[]{:S(2)}) copy-start(bf16[1,56,128,128]{3,2,1,0:T(8,128)(2,1)} %param.8) | copy-start | bytes 5505028
  7.2 29.3 %collective-permute-start.1 = (bf16[64,2048]{1,0:T(8,128)(2,1)}, bf16[64,2048]{1,0:T(8,128)(2,1)S(1)}, u32[]{:S(2)}, u32[]{:S(2)}) collective-permute-start(bf16[64,2048]{1,0:T(8,128)(2,1)} %param.7), channel_id=1, source_target_pairs={{0,2},{1,3},{2,0},{3,1},{4,6},{5,7},{6,4},{7,5},{8,10},{9,11},{10,... | collective-permute-start | bytes 786440 | tf_op jit(solution)/shard_map/ppermute | solution.py:10
  13.1 23.5 %collective-permute-start = (bf16[64,2048]{1,0:T(8,128)(2,1)}, bf16[64,2048]{1,0:T(8,128)(2,1)S(1)}, u32[]{:S(2)}, u32[]{:S(2)}) collective-permute-start(bf16[64,2048]{1,0:T(8,128)(2,1)} %param.7), channel_id=1, source_target_pairs={{0,1},{1,0},{2,3},{3,2},{4,5},{5,4},{6,7},{7,6},{8,9},{9,8},{10,11... | collective-permute-start | bytes 786440 | tf_op jit(solution)/shard_map/ppermute | solution.py:10
  16.6 30.2 %collective-permute-start.3 = (bf16[64,2048]{1,0:T(8,128)(2,1)}, bf16[64,2048]{1,0:T(8,128)(2,1)S(1)}, u32[]{:S(2)}, u32[]{:S(2)}) collective-permute-start(bf16[64,2048]{1,0:T(8,128)(2,1)} %param.7), channel_id=1, source_target_pairs={{0,8},{1,9},{2,10},{3,11},{4,12},{5,13},{6,14},{7,15},{8,0},{9,1},... | collective-permute-start | bytes 786440 | tf_op jit(solution)/shard_map/ppermute | solution.py:10
  29.4 49.4 %collective-permute-start.2 = (bf16[64,2048]{1,0:T(8,128)(2,1)}, bf16[64,2048]{1,0:T(8,128)(2,1)S(1)}, u32[]{:S(2)}, u32[]{:S(2)}) collective-permute-start(bf16[64,2048]{1,0:T(8,128)(2,1)} %param.7), channel_id=1, source_target_pairs={{0,4},{1,5},{2,6},{3,7},{4,0},{5,1},{6,2},{7,3},{8,12},{9,13},{10,... | collective-permute-start | bytes 786440 | tf_op jit(solution)/shard_map/ppermute | solution.py:10
  84.0 1.4 copy-start.3
  85.4 6.2 copy-start.2
  86.0 12.1 %copy-start.1 = (bf16[512,512]{1,0:T(8,128)(2,1)S(1)}, bf16[512,512]{1,0:T(8,128)(2,1)}, u32[]{:S(2)}) copy-start(bf16[512,512]{1,0:T(8,128)(2,1)} %param.12) | copy-start | bytes 1572868
  86.9 11.3 %all-to-all-start = ((bf16[64,8,256]{2,0,1:T(8,128)(2,1)}), bf16[64,8,256]{2,0,1:T(8,128)(2,1)S(1)}, u32[]{:S(2)}, u32[]{:S(2)}) async-start(bf16[64,8,256]{2,0,1:T(8,128)(2,1)} %copy.75), calls=%async_computation | async-start | bytes 524288 | tf_op jit(solution)/shard_map/all_to_all | solution.py:67
  99.4 5.6 copy-start.4
  100.6 10.9 %all-to-all-start.1 = ((bf16[8,64,256]{2,1,0:T(8,128)(2,1)}), bf16[8,64,256]{2,1,0:T(8,128)(2,1)S(1)}, u32[]{:S(2)}, u32[]{:S(2)}) async-start(bf16[8,64,256]{2,1,0:T(8,128)(2,1)} %bitcast.12), calls=%async_computation.1 | async-start | bytes 524288 | tf_op jit(solution)/shard_map/all_to_all | solution.py:79
  104.9 514.8 %all-reduce.2.cloned.1.call-start = ((), (), s32[]{:S(2)}) async-start(), calls=%async_computation.2 | async-start | bytes 2097152 | tf_op jit(solution)/shard_map/psum | solution.py:75
  126.3 21.3 %collective-permute-start.5 = (bf16[64,2048]{1,0:T(8,128)(2,1)}, bf16[64,2048]{1,0:T(8,128)(2,1)}, u32[]{:S(2)}, u32[]{:S(2)}) collective-permute-start(bf16[64,2048]{1,0:T(8,128)(2,1)} %bitcast.96), channel_id=1, source_target_pairs={{0,2},{1,3},{2,0},{3,1},{4,6},{5,7},{6,4},{7,5},{8,10},{9,11},{10,... | collective-permute-start | bytes 786440 | tf_op jit(solution)/shard_map/ppermute | solution.py:10
  128.3 52.9 %collective-permute-start.6 = (bf16[64,2048]{1,0:T(8,128)(2,1)}, bf16[64,2048]{1,0:T(8,128)(2,1)}, u32[]{:S(2)}, u32[]{:S(2)}) collective-permute-start(bf16[64,2048]{1,0:T(8,128)(2,1)} %bitcast.95), channel_id=1, source_target_pairs={{0,4},{1,5},{2,6},{3,7},{4,0},{5,1},{6,2},{7,3},{8,12},{9,13},{10,... | collective-permute-start | bytes 786440 | tf_op jit(solution)/shard_map/ppermute | solution.py:10
  130.2 50.9 %collective-permute-start.7 = (bf16[64,2048]{1,0:T(8,128)(2,1)S(1)}, bf16[64,2048]{1,0:T(8,128)(2,1)}, u32[]{:S(2)}, u32[]{:S(2)}) collective-permute-start(bf16[64,2048]{1,0:T(8,128)(2,1)S(1)} %bitcast.108), channel_id=1, source_target_pairs={{0,8},{1,9},{2,10},{3,11},{4,12},{5,13},{6,14},{7,15},{8,0},{9,1},... | collective-permute-start | bytes 786440 | tf_op jit(solution)/shard_map/ppermute | solution.py:10
  138.7 42.4 %collective-permute-start.4 = (bf16[64,2048]{1,0:T(8,128)(2,1)S(1)}, bf16[64,2048]{1,0:T(8,128)(2,1)}, u32[]{:S(2)}, u32[]{:S(2)}) collective-permute-start(bf16[64,2048]{1,0:T(8,128)(2,1)S(1)} %bitcast.107), channel_id=1, source_target_pairs={{0,1},{1,0},{2,3},{3,2},{4,5},{5,4},{6,7},{7,6},{8,9},{9,8},{10,11... | collective-permute-start | bytes 786440 | tf_op jit(solution)/shard_map/ppermute | solution.py:10
  145.8 35.3 %slice-start = ((f32[64,5,2048]{2,1,0:T(8,128)}), f32[64,1,2048]{2,1,0:T(1,128)S(1)}, s32[]{:S(2)}) async-start(f32[64,5,2048]{2,1,0:T(8,128)} %reshape.232), calls=%async_computation.3 | async-start | bytes 1048576 | tf_op jit(solution)/shard_map/slice | solution.py:87
Sparse Core Ops, SparseCore 0:
  146.0 473.7 all-reduce.1
where the time goes:
time: 630 us; the launch traced here: 629 us
  waiting for transfers between devices  525 us (83%)
  starting transfers between devices  53.5 us (8%)
  local copies, waits for them, and re-layouts  22.5 us (4%)
  between operations  14.9 us (2%)
  matrix products  7.74 us (1%)
    psum x1, waiting for transfers between devices, body(): weight_gradient = lax.psum(weight_term, ('feat', 'vert'))  436 us
    ppermute x8, waiting for transfers between devices, partner(): lax.ppermute(shard, axis, [(i, i ^ 1 << stride) for i in range(lax.axis_s...  75.5 us
    ppermute x8, starting transfers between devices, partner(): lax.ppermute(shard, axis, [(i, i ^ 1 << stride) for i in range(lax.axis_s...  44.3 us
  transfers between devices with their start and end apart: 11, of which 6 were waited for; matrix products, arithmetic and copies ran while one was open for 1% of the time, Pallas kernels for 0%

commit v1 on v0

--- a/solution.py
+++ b/solution.py
@@ -72,7 +72,7 @@
         jnp.bfloat16
     )
     weight_term = jnp.einsum("iv,ov->io", full_rows, pre_grad, preferred_element_type=jnp.float32)
-    weight_gradient = lax.psum(weight_term, ("feat", "vert"))
+    weight_gradient = lax.psum(lax.psum(weight_term, "vert"), "feat")
     agg_grad = jnp.einsum("io,ov->iv", weight, pre_grad, preferred_element_type=jnp.float32).astype(
         jnp.bfloat16
     )

time: 630 us -> 499 us (0.79)
  waiting for transfers between devices: 525 us -> 393 us
    psum x1 -> x2, waiting for transfers between devices: 436 us -> 340 us  [body(): weight_gradient = lax.psum(lax.psum(weight_term, 'vert'), 'feat')]
    ppermute x8, waiting for transfers between devices: 75.5 us -> 41.4 us  [partner(): lax.ppermute(shard, axis, [(i, i ^ 1 << stride) for i in range(lax.axis_s...]
  transfers between devices with their start and end apart: 11 -> 12, of which waited for: 6 -> 6; matrix products, arithmetic and copies ran while one was open for 1% -> 5% of each run, Pallas kernels for 0% -> 0%
where the time goes in v1:
time: 499 us; the launch traced here: 497 us
  waiting for transfers between devices  393 us (79%)
  starting transfers between devices  53.5 us (11%)
  local copies, waits for them, and re-layouts  22.5 us (5%)
  between operations  15 us (3%)
  matrix products  7.74 us (2%)
  other arithmetic  5.94 us (1%)
    psum x2, waiting for transfers between devices, body(): weight_gradient = lax.psum(lax.psum(weight_term, 'vert'), 'feat')  340 us
    ppermute x8, starting transfers between devices, partner(): lax.ppermute(shard, axis, [(i, i ^ 1 << stride) for i in range(lax.axis_s...  44.3 us
    ppermute x8, waiting for transfers between devices, partner(): lax.ppermute(shard, axis, [(i, i ^ 1 << stride) for i in range(lax.axis_s...  41.4 us
    unnamed x26, local copies, waits for them, and re-layouts  10.5 us
  transfers between devices with their start and end apart: 12, of which 6 were waited for; matrix products, arithmetic and copies ran while one was open for 5% of the time, Pallas kernels for 0%

profile of v1, /device:TPU:1, one launch (start us, length us, event | category | flops | bytes accessed | tf_op | source)
XLA Modules:
  0.0 497.2 jit_solution(14834941330735500032)
XLA Ops:
  7.2 0.0 copy-start
  7.2 5.9 %collective-permute-start.1 = (bf16[64,2048]{1,0:T(8,128)(2,1)}, bf16[64,2048]{1,0:T(8,128)(2,1)S(1)}, u32[]{:S(2)}, u32[]{:S(2)}) collective-permute-start(bf16[64,2048]{1,0:T(8,128)(2,1)} %param.7), channel_id=1, source_target_pairs={{0,2},{1,3},{2,0},{3,1},{4,6},{5,7},{6,4},{7,5},{8,10},{9,11},{10,... | collective-permute-start | bytes 786440 | tf_op jit(solution)/shard_map/ppermute | solution.py:10
  13.1 3.5 collective-permute-start
  16.6 12.7 %collective-permute-start.3 = (bf16[64,2048]{1,0:T(8,128)(2,1)}, bf16[64,2048]{1,0:T(8,128)(2,1)S(1)}, u32[]{:S(2)}, u32[]{:S(2)}) collective-permute-start(bf16[64,2048]{1,0:T(8,128)(2,1)} %param.7), channel_id=1, source_target_pairs={{0,8},{1,9},{2,10},{3,11},{4,12},{5,13},{6,14},{7,15},{8,0},{9,1},... | collective-permute-start | bytes 786440 | tf_op jit(solution)/shard_map/ppermute | solution.py:10
  29.4 4.0 collective-permute-start.2
  34.0 0.7 fusion.47
  34.7 0.7 fusion.49
  35.4 1.0 copy.87
  36.4 0.8 copy_dynamic-update-slice_fusion.4
  37.1 0.0 collective-permute-done.1
  37.2 0.0 collective-permute-done
  37.2 9.6 %collective-permute-done.3 = bf16[64,2048]{1,0:T(8,128)(2,1)S(1)} collective-permute-done((bf16[64,2048]{1,0:T(8,128)(2,1)}, bf16[64,2048]{1,0:T(8,128)(2,1)S(1)}, u32[]{:S(2)}, u32[]{:S(2)}) %collective-permute-start.3) | collective-permute-done | bytes 262176 | tf_op jit(solution)/shard_map/ppermute | solution.py:10
  46.9 31.9 %collective-permute-done.2 = bf16[64,2048]{1,0:T(8,128)(2,1)S(1)} collective-permute-done((bf16[64,2048]{1,0:T(8,128)(2,1)}, bf16[64,2048]{1,0:T(8,128)(2,1)S(1)}, u32[]{:S(2)}, u32[]{:S(2)}) %collective-permute-start.2) | collective-permute-done | bytes 262176 | tf_op jit(solution)/shard_map/ppermute | solution.py:10
  78.8 0.8 copy_dynamic-update-slice_fusion.3
  79.5 0.8 copy_dynamic-update-slice_fusion.2
  80.3 0.8 copy_dynamic-update-slice_fusion.1
  81.0 0.8 copy_dynamic-update-slice_fusion
  81.8 2.2 gather_fusion
  84.0 0.0 copy-done
  84.0 0.0 copy-start.3
  84.1 1.4 fusion.2
  85.4 0.0 copy-done.3
  85.4 0.0 copy-start.2
  85.4 0.6 fusion.18
  86.0 0.1 convert_element_type.72
  86.1 0.8 copy.75
  86.9 4.8 all-to-all-start
  91.7 0.1 copy.76
  91.9 6.3 %all-to-all-done = bf16[64,8,256]{2,0,1:T(8,128)(2,1)S(1)} async-done(((bf16[64,8,256]{2,0,1:T(8,128)(2,1)}), bf16[64,8,256]{2,0,1:T(8,128)(2,1)S(1)}, u32[]{:S(2)}, u32[]{:S(2)}) %all-to-all-start) | async-done | bytes 262176 | tf_op jit(solution)/shard_map/all_to_all | solution.py:67
  98.2 1.2 multiply_convert_fusion
  99.4 0.3 fusion.17
  99.7 0.8 copy.77
  100.6 4.4 all-to-all-start.1
  104.9 1.3 fusion.52
  106.2 0.0 all-reduce.3.cloned.1.call-update
  106.2 0.0 all-reduce.5.cloned.1.call-start
  106.3 5.2 %all-to-all-done.1 = bf16[8,64,256]{2,1,0:T(8,128)(2,1)S(1)} async-done(((bf16[8,64,256]{2,1,0:T(8,128)(2,1)}), bf16[8,64,256]{2,1,0:T(8,128)(2,1)S(1)}, u32[]{:S(2)}, u32[]{:S(2)}) %all-to-all-start.1) | async-done | bytes 262176 | tf_op jit(solution)/shard_map/all_to_all | solution.py:79
  111.5 0.1 copy.78
  111.6 0.1 reshape.231
  111.7 0.1 copy.79
  111.8 0.7 gather_fusion.1
  112.5 0.6 fusion.11
  113.1 2.4 fusion.8
  115.5 4.4 reshape.232
  119.9 2.6 convert.6
  122.4 1.9 fusion.51
  124.4 0.2 copy.115
  124.5 0.2 copy.112
  124.7 0.9 copy.113
  125.5 0.8 copy.114
  126.4 1.9 collective-permute-start.5
  128.3 1.9 collective-permute-start.6
  130.2 8.5 %collective-permute-start.7 = (bf16[64,2048]{1,0:T(8,128)(2,1)S(1)}, bf16[64,2048]{1,0:T(8,128)(2,1)}, u32[]{:S(2)}, u32[]{:S(2)}) collective-permute-start(bf16[64,2048]{1,0:T(8,128)(2,1)S(1)} %bitcast.108), channel_id=1, source_target_pairs={{0,8},{1,9},{2,10},{3,11},{4,12},{5,13},{6,14},{7,15},{8,0},{9,1},... | collective-permute-start | bytes 786440 | tf_op jit(solution)/shard_map/ppermute | solution.py:10
  138.7 5.8 %collective-permute-start.4 = (bf16[64,2048]{1,0:T(8,128)(2,1)S(1)}, bf16[64,2048]{1,0:T(8,128)(2,1)}, u32[]{:S(2)}, u32[]{:S(2)}) collective-permute-start(bf16[64,2048]{1,0:T(8,128)(2,1)S(1)} %bitcast.107), channel_id=1, source_target_pairs={{0,1},{1,0},{2,3},{3,2},{4,5},{5,4},{6,7},{7,6},{8,9},{9,8},{10,11... | collective-permute-start | bytes 786440 | tf_op jit(solution)/shard_map/ppermute | solution.py:10
  144.5 260.4 %all-reduce.3.cloned.1.call-done = f32[512,512]{1,0:T(8,128)} async-done(((f32[512,512]{1,0:T(8,128)}), f32[512,512]{1,0:T(8,128)}) %all-reduce.3.cloned.1.call-update) | async-done | bytes 1048592 | tf_op jit(solution)/shard_map/psum | solution.py:75
  404.9 0.0 all-reduce.5.cloned.1.call-update
  404.9 1.8 copy.81
  406.8 0.0 collective-permute-done.5
  406.8 0.0 collective-permute-done.6
  406.8 0.0 collective-permute-done.7
  406.8 0.0 collective-permute-done.4
  406.8 2.0 fusion.25
  408.8 79.2 %all-reduce.5.cloned.1.call-done = f32[512,512]{1,0:T(8,128)} async-done(((f32[512,512]{1,0:T(8,128)}), f32[512,512]{1,0:T(8,128)}) %all-reduce.5.cloned.1.call-update) | async-done | bytes 1048592 | tf_op jit(solution)/shard_map/psum | solution.py:75
  488.1 2.3 copy.123
  (15 shorter events, 0.2 us)
Async XLA Ops:
  7.2 76.9 %copy-start = (bf16[1,56,128,128]{3,2,1,0:T(8,128)(2,1)S(1)}, bf16[1,56,128,128]{3,2,1,0:T(8,128)(2,1)}, u32[]{:S(2)}) copy-start(bf16[1,56,128,128]{3,2,1,0:T(8,128)(2,1)} %param.8) | copy-start | bytes 5505028
  7.2 30.0 %collective-permute-start.1 = (bf16[64,2048]{1,0:T(8,128)(2,1)}, bf16[64,2048]{1,0:T(8,128)(2,1)S(1)}, u32[]{:S(2)}, u32[]{:S(2)}) collective-permute-start(bf16[64,2048]{1,0:T(8,128)(2,1)} %param.7), channel_id=1, source_target_pairs={{0,2},{1,3},{2,0},{3,1},{4,6},{5,7},{6,4},{7,5},{8,10},{9,11},{10,... | collective-permute-start | bytes 786440 | tf_op jit(solution)/shard_map/ppermute | solution.py:10
  13.1 24.1 %collective-permute-start = (bf16[64,2048]{1,0:T(8,128)(2,1)}, bf16[64,2048]{1,0:T(8,128)(2,1)S(1)}, u32[]{:S(2)}, u32[]{:S(2)}) collective-permute-start(bf16[64,2048]{1,0:T(8,128)(2,1)} %param.7), channel_id=1, source_target_pairs={{0,1},{1,0},{2,3},{3,2},{4,5},{5,4},{6,7},{7,6},{8,9},{9,8},{10,11... | collective-permute-start | bytes 786440 | tf_op jit(solution)/shard_map/ppermute | solution.py:10
  16.6 30.2 %collective-permute-start.3 = (bf16[64,2048]{1,0:T(8,128)(2,1)}, bf16[64,2048]{1,0:T(8,128)(2,1)S(1)}, u32[]{:S(2)}, u32[]{:S(2)}) collective-permute-start(bf16[64,2048]{1,0:T(8,128)(2,1)} %param.7), channel_id=1, source_target_pairs={{0,8},{1,9},{2,10},{3,11},{4,12},{5,13},{6,14},{7,15},{8,0},{9,1},... | collective-permute-start | bytes 786440 | tf_op jit(solution)/shard_map/ppermute | solution.py:10
  29.4 49.4 %collective-permute-start.2 = (bf16[64,2048]{1,0:T(8,128)(2,1)}, bf16[64,2048]{1,0:T(8,128)(2,1)S(1)}, u32[]{:S(2)}, u32[]{:S(2)}) collective-permute-start(bf16[64,2048]{1,0:T(8,128)(2,1)} %param.7), channel_id=1, source_target_pairs={{0,4},{1,5},{2,6},{3,7},{4,0},{5,1},{6,2},{7,3},{8,12},{9,13},{10,... | collective-permute-start | bytes 786440 | tf_op jit(solution)/shard_map/ppermute | solution.py:10
  84.0 1.4 copy-start.3
  85.4 6.3 %copy-start.2 = (bf16[512,256]{1,0:T(8,128)(2,1)S(1)}, bf16[512,256]{1,0:T(8,128)(2,1)}, u32[]{:S(2)}) copy-start(bf16[512,256]{1,0:T(8,128)(2,1)} %param.13) | copy-start | bytes 786436
  86.0 5.8 %copy-start.4 = (s32[1,56]{1,0:T(1,128)S(1)}, s32[1,56]{1,0:T(1,128)}, u32[]{:S(2)}) copy-start(s32[1,56]{1,0:T(1,128)} %param.10) | copy-start | bytes 676
  86.0 12.2 %copy-start.1 = (bf16[512,512]{1,0:T(8,128)(2,1)S(1)}, bf16[512,512]{1,0:T(8,128)(2,1)}, u32[]{:S(2)}) copy-start(bf16[512,512]{1,0:T(8,128)(2,1)} %param.12) | copy-start | bytes 1572868
  86.9 11.3 %all-to-all-start = ((bf16[64,8,256]{2,0,1:T(8,128)(2,1)}), bf16[64,8,256]{2,0,1:T(8,128)(2,1)S(1)}, u32[]{:S(2)}, u32[]{:S(2)}) async-start(bf16[64,8,256]{2,0,1:T(8,128)(2,1)} %copy.75), calls=%async_computation | async-start | bytes 524288 | tf_op jit(solution)/shard_map/all_to_all | solution.py:67
  100.6 10.9 %all-to-all-start.1 = ((bf16[8,64,256]{2,1,0:T(8,128)(2,1)}), bf16[8,64,256]{2,1,0:T(8,128)(2,1)S(1)}, u32[]{:S(2)}, u32[]{:S(2)}) async-start(bf16[8,64,256]{2,1,0:T(8,128)(2,1)} %bitcast.12), calls=%async_computation.1 | async-start | bytes 524288 | tf_op jit(solution)/shard_map/all_to_all | solution.py:79
  104.9 300.0 %all-reduce.3.cloned.1.call-start = ((), (), s32[]{:S(2)}) async-start(), calls=%async_computation.2 | async-start | bytes 2097152 | tf_op jit(solution)/shard_map/psum | solution.py:75
  106.2 381.8 %all-reduce.5.cloned.1.call-start = ((), (), s32[]{:S(2)}) async-start(), calls=%async_computation.3 | async-start | bytes 2097152 | tf_op jit(solution)/shard_map/psum | solution.py:75
  126.4 280.4 %collective-permute-start.5 = (bf16[64,2048]{1,0:T(8,128)(2,1)}, bf16[64,2048]{1,0:T(8,128)(2,1)S(1)}, u32[]{:S(2)}, u32[]{:S(2)}) collective-permute-start(bf16[64,2048]{1,0:T(8,128)(2,1)} %bitcast.96), channel_id=1, source_target_pairs={{0,2},{1,3},{2,0},{3,1},{4,6},{5,7},{6,4},{7,5},{8,10},{9,11},{10,... | collective-permute-start | bytes 786440 | tf_op jit(solution)/shard_map/ppermute | solution.py:10
  128.3 278.5 %collective-permute-start.6 = (bf16[64,2048]{1,0:T(8,128)(2,1)}, bf16[64,2048]{1,0:T(8,128)(2,1)S(1)}, u32[]{:S(2)}, u32[]{:S(2)}) collective-permute-start(bf16[64,2048]{1,0:T(8,128)(2,1)} %bitcast.95), channel_id=1, source_target_pairs={{0,4},{1,5},{2,6},{3,7},{4,0},{5,1},{6,2},{7,3},{8,12},{9,13},{10,... | collective-permute-start | bytes 786440 | tf_op jit(solution)/shard_map/ppermute | solution.py:10
  130.2 276.6 %collective-permute-start.7 = (bf16[64,2048]{1,0:T(8,128)(2,1)S(1)}, bf16[64,2048]{1,0:T(8,128)(2,1)}, u32[]{:S(2)}, u32[]{:S(2)}) collective-permute-start(bf16[64,2048]{1,0:T(8,128)(2,1)S(1)} %bitcast.108), channel_id=1, source_target_pairs={{0,8},{1,9},{2,10},{3,11},{4,12},{5,13},{6,14},{7,15},{8,0},{9,1},... | collective-permute-start | bytes 786440 | tf_op jit(solution)/shard_map/ppermute | solution.py:10
  138.7 268.1 %collective-permute-start.4 = (bf16[64,2048]{1,0:T(8,128)(2,1)S(1)}, bf16[64,2048]{1,0:T(8,128)(2,1)}, u32[]{:S(2)}, u32[]{:S(2)}) collective-permute-start(bf16[64,2048]{1,0:T(8,128)(2,1)S(1)} %bitcast.107), channel_id=1, source_target_pairs={{0,1},{1,0},{2,3},{3,2},{4,5},{5,4},{6,7},{7,6},{8,9},{9,8},{10,11... | collective-permute-start | bytes 786440 | tf_op jit(solution)/shard_map/ppermute | solution.py:10
  404.9 1.9 slice-start
Sparse Core Ops, SparseCore 0:
  109.7 295.1 all-reduce.2
  407.4 80.6 all-reduce.4
